TPU v7x, 512 devices: a whole 4x8x8 slice. The times are simulated.
512 devices in a mesh: pair: 16 (over z_lo, y), row: 4 (over x), col: 8 (over z_hi, core).
Axes of the slice: x: 4, y: 8, z: 8 (z_hi: 4, z_lo: 2; z = z_hi * 2 + z_lo), core: 2. Of those that a mesh axis runs over, the one named last changes fastest.
Arguments:
- integrals: bfloat16 [12288, 4096], P(('pair', 'col')), may hold values from -0.21875 to 0.21875
- inverse_factor: bfloat16 [4096, 4096], P('row', ('pair', 'col')), may hold values from -4 to 4, as said below
- energies: float32 [12288], P('pair'), may hold values from 0.25 to 8
- frequency: float32 [1], replicated, may hold values from 0.5 to 2
Outputs:
- response: float32 [4096, 4096], P(('row', 'pair'), 'col')
Inputs may be any that keep to these rules, and one draw needn't show every extreme that they name: `inverse_factor`: zero above the diagonal; the diagonal lies between 0.5 and 3.
All inputs are finite; a program needn't handle non-finite values.
Results may differ from a plain program's by a relative error of at most 0.0025.
Values may be sent and summed in bfloat16 or wider, within the bound.
A program may use at most 64 MiB of HBM per device.

v0:
```python
import jax
import jax.numpy as jnp
from jax import lax
from jax.sharding import PartitionSpec as P


def contract(x_columns, portion):
    return lax.dot_general(
        x_columns, portion, (((1,), (1,)), ((), ())), preferred_element_type=jnp.float32
    )


def on_device(integrals, inverse_factor, energies, frequency):
    n_col = lax.axis_size("col")
    aux_width = integrals.shape[1]
    q_cols = aux_width // n_col
    local_rows = contract(
        integrals, lax.all_gather(inverse_factor, ("pair", "col"), axis=1, tiled=True)
    )
    group_b = lax.all_gather(local_rows.astype(jnp.bfloat16), "col", axis=0, tiled=True)
    col_position = lax.axis_index("col")
    empty = jnp.zeros((group_b.shape[0], q_cols), jnp.bfloat16)
    portion = lax.all_gather(group_b, "row", axis=1, tiled=True)
    portion_width = portion.shape[1]
    wanted = col_position * q_cols + jnp.arange(q_cols, dtype=jnp.int32)
    inside = (wanted >= 0) & (wanted < portion_width)
    selected = jnp.take(portion, jnp.clip(wanted, 0, portion_width - 1), axis=1)
    col_b = jnp.where(inside[None, :], selected, empty)
    factor = 2.0 * energies / (energies * energies + frequency[0] * frequency[0])
    scaled = (factor[:, None] * group_b.astype(jnp.float32)).astype(jnp.bfloat16)
    return lax.psum_scatter(
        lax.dot_general(
            scaled, col_b, (((0,), (0,)), ((), ())), preferred_element_type=jnp.float32
        ),
        "pair",
        scatter_dimension=0,
        tiled=True,
    )


def solution(mesh):
    return jax.shard_map(
        on_device,
        mesh=mesh,
        in_specs=(P(("pair", "col"), None), P("row", ("pair", "col")), P("pair"), P()),
        out_specs=P(("row", "pair"), "col"),
        check_vma=False,
    )
```

profile of v0, /device:TPU:4, one launch (start us, length us, event | category | flops | bytes accessed | tf_op | source)
XLA Modules:
  0.0 452.1 jit_solution(15941670298254573152)
XLA Ops:
  6.5 0.0 copy-start
  6.5 0.0 all-gather.4.cloned.1.call-start
  6.5 0.7 all-gather.4.cloned.1.call-update
  7.3 0.0 copy-start.2
  7.3 0.0 all-gather.6.cloned.1.call-start
  7.3 231.1 %all-gather.4.cloned.1.call-done = bf16[1024,4096]{0,1:T(8,128)(2,1)} async-done(((bf16[1024,32]{0,1:T(8,128)(2,1)}), bf16[1024,4096]{0,1:T(8,128)(2,1)}) %all-gather.4.cloned.1.call-update) | async-done | bytes 8388624 | tf_op jit(solution)/shard_map/all_gather | solution.py:18
  238.4 0.0 copy-done
  238.4 5.5 %convolution_convert_fusion = bf16[96,1024]{1,0:T(8,128)(2,1)} fusion(bf16[96,4096]{1,0:T(8,128)(2,1)S(1)} %copy-done, bf16[1024,4096]{0,1:T(8,128)(2,1)} %all-gather.4.cloned.1.call-done), kind=kOutput, calls=%fused_computation.4 | convolution fusion | flops 805404672 | bytes 9371648 | tf_op jit(solution)/shard_map/dot_general | solution.py:8
  243.9 0.0 all-gather.6.cloned.1.call-update
  243.9 0.0 all-gather.8.cloned.1.call-start
  244.0 35.1 %all-gather.6.cloned.1.call-done = bf16[768,1024]{1,0:T(8,128)(2,1)} async-done(((bf16[96,1024]{1,0:T(8,128)(2,1)}), bf16[768,1024]{1,0:T(8,128)(2,1)}) %all-gather.6.cloned.1.call-update) | async-done | bytes 1572880 | tf_op jit(solution)/shard_map/all_gather | solution.py:20
  279.0 0.0 all-gather.8.cloned.1.call-update
  279.1 0.0 reduce-scatter.2.cloned.1.call-start
  279.8 0.0 copy-done.2
  279.8 69.9 %all-gather.8.cloned.1.call-done = bf16[768,4096]{1,0:T(8,128)(2,1)} async-done(((bf16[768,1024]{1,0:T(8,128)(2,1)}), bf16[768,4096]{1,0:T(8,128)(2,1)}) %all-gather.8.cloned.1.call-update) | async-done | bytes 6291472 | tf_op jit(solution)/shard_map/all_gather | solution.py:23
  349.8 8.7 %copy.6 = bf16[768,4096]{0,1:T(8,128)(2,1)} copy(bf16[768,4096]{1,0:T(8,128)(2,1)} %all-gather.8.cloned.1.call-done) | data formatting | bytes 12582912 | tf_op jit(solution)/shard_map/all_gather | solution.py:23
  358.4 0.0 copy-start.1
  358.4 6.1 %gather_fusion = bf16[512,768]{1,0:T(8,128)(2,1)S(1)} fusion(bf16[768,4096]{0,1:T(8,128)(2,1)} %copy.6, s32[1024]{0:T(1024)S(1)} %pad_clamp_fusion), kind=kCustom, calls=%fused_computation | custom fusion | bytes 1574912 | tf_op jit(solution)/shard_map/jit(_take)/gather | solution.py:27
  364.6 0.0 copy-done.1
  364.6 2.7 fusion
  367.2 0.0 reduce-scatter.2.cloned.1.call-update
  367.2 78.3 %reduce-scatter.2.cloned.1.call-done = f32[64,512]{1,0:T(8,128)} async-done(((f32[1024,512]{1,0:T(8,128)}), f32[64,512]{1,0:T(8,128)}) %reduce-scatter.2.cloned.1.call-update) | async-done | bytes 131088 | tf_op jit(solution)/shard_map/reduce_scatter | solution.py:31
  (4 shorter events, 0.0 us)
Async XLA Ops:
  6.5 231.8 %copy-start = (bf16[96,4096]{1,0:T(8,128)(2,1)S(1)}, bf16[96,4096]{1,0:T(8,128)(2,1)}, u32[]{:S(2)}) copy-start(bf16[96,4096]{1,0:T(8,128)(2,1)} %param.4) | copy-start | bytes 2359300
  6.5 231.8 %all-gather.4.cloned.1.call-start = ((), (), s32[]{:S(2)}) async-start(), calls=%async_computation.1 | async-start | bytes 8454144 | tf_op jit(solution)/shard_map/all_gather | solution.py:18
  7.3 272.6 %copy-start.2 = (f32[768]{0:T(1024)S(1)}, f32[768]{0:T(1024)}, u32[]{:S(2)}) copy-start(f32[768]{0:T(1024)} %param.6) | copy-start | bytes 9220
  7.3 271.8 %all-gather.6.cloned.1.call-start = ((), (), s32[]{:S(2)}) async-start(), calls=%async_computation.2 | async-start | bytes 1769472 | tf_op jit(solution)/shard_map/all_gather | solution.py:20
  243.9 105.9 %all-gather.8.cloned.1.call-start = ((), (), s32[]{:S(2)}) async-start(), calls=%async_computation.3 | async-start | bytes 7864320 | tf_op jit(solution)/shard_map/all_gather | solution.py:23
  279.1 166.5 %reduce-scatter.2.cloned.1.call-start = ((), (), s32[]{:S(2)}) async-start(), calls=%async_computation.4 | async-start | bytes 2228224 | tf_op jit(solution)/shard_map/reduce_scatter | solution.py:31
  358.4 6.1 %copy-start.1 = (bf16[768,1024]{1,0:T(8,128)(2,1)S(1)}, bf16[768,1024]{1,0:T(8,128)(2,1)}, u32[]{:S(2)}) copy-start(bf16[768,1024]{1,0:T(8,128)(2,1)} %all-gather.6.cloned.1.call-done) | copy-start | bytes 4718596
Sparse Core Ops, SparseCore 0:
  9.5 228.8 all-gather.3
  244.1 34.9 all-gather.5
  281.1 68.5 all-gather.7
  367.4 78.1 reduce-scatter.1
where the time goes:
time: 452 us
  waiting for transfers between devices  415 us (92%)
  local copies, waits for them, and re-layouts  14.8 us (3%)
  between operations  13.8 us (3%)
  matrix products  8.18 us (2%)
    all_gather x1, waiting for transfers between devices, on_device(): lax.all_gather(inverse_factor, ('pair', 'col'), axis=1, tiled=True)  231 us
    reduce_scatter x1, waiting for transfers between devices, on_device(): lax.psum_scatter(lax.dot_general(scaled, col_b, (((0,), (0,)), ((), ())),...  78.3 us
    all_gather x1, waiting for transfers between devices, on_device(): portion = lax.all_gather(group_b, 'row', axis=1, tiled=True)  69.9 us
    all_gather x1, waiting for transfers between devices, on_device(): lax.all_gather(local_rows.astype(jnp.bfloat16), 'col', axis=0, tiled=True)  35.1 us
  transfers between devices with their start and end apart: 4, of which 4 were waited for; matrix products, arithmetic and copies ran while one was open for 0% of the time, Pallas kernels for 0%

commit v1 on v0

v1 whole, which is shorter than its diff:
```python
import functools

import jax
import jax.numpy as jnp
from jax import lax
from jax.experimental import pallas as pl
from jax.experimental.pallas import tpu as pltpu
from jax.sharding import PartitionSpec as P

MESH = pl.DeviceIdType.MESH
F32, BF16 = jnp.float32, jnp.bfloat16
LAG = 2
NARROW_TERMS = 2


def rem(a, b):
    return lax.rem(a, jnp.int32(b))


def div(a, b):
    return lax.div(a, jnp.int32(b))


def device(x, y, z, c):
    return {"pair": rem(z, 2) * 8 + y, "row": x, "col": div(z, 2) * 2 + c}


def kernel(
    i_ref, l_ref, e_ref, f_ref, out_ref,
    lbuf, i2, tacc, tr, tc, eall, fcol, r, sb16, sb32, rb16, rb32, res,
    init_s, init_r, i_s, i_r, e_s, e_r,
    a1_s, a1_r, b1_s, b1_r, a2_s, a2_r, b2_s, b2_r,
    z_s, z_r, x_s, c_s, x_r, y_s, y_r, o_s, o_r,
):
    pair, x, col = lax.axis_index("pair"), lax.axis_index("row"), lax.axis_index("col")
    zlo, y = div(pair, 8), rem(pair, 8)
    zhi, c = div(col, 2), rem(col, 2)
    z = zhi * 2 + zlo
    j = jnp.where(c == 0, x, 7 - x)
    sibling = device(x, y, z, 1 - c)
    x_next, x_prev = device(rem(x + 1, 4), y, z, c), device(rem(x + 3, 4), y, z, c)
    y_side = (device(x, rem(y + 1, 8), z, c), device(x, rem(y + 7, 8), z, c))
    z_side = (device(x, y, rem(z + 1, 8), c), device(x, y, rem(z + 7, 8), c))
    z_pair = zhi * 2 + 1 - zlo

    def remote(src, dst, ssem, rsem, dev):
        return pltpu.make_async_remote_copy(
            src_ref=src, dst_ref=dst, send_sem=ssem, recv_sem=rsem,
            device_id=dev, device_id_type=MESH)

    barrier = pltpu.get_barrier_semaphore()
    for k in range(1, 16):
        dx, dz, dc = k // 4, (k // 2) % 2, k % 2
        pl.semaphore_signal(
            barrier, inc=1, device_id_type=MESH,
            device_id=device(rem(x + dx, 4), y, zhi * 2 + rem(zlo + dz, 2), rem(c + dc, 2)))
    z_out = jnp.where(zlo == 1, rem(z + 1, 8), rem(z + 7, 8))
    for dev in (*y_side, device(x, y, z_out, c)):
        pl.semaphore_signal(barrier, inc=1, device_id_type=MESH, device_id=dev)
    pl.semaphore_wait(barrier, 18)

    def need(block, zl, yy):
        return zl * 4 + div(yy, 2) <= block

    def init_copies(t, h, act):
        block = 2 * x + t
        ox = jnp.where(block < 4, block, 7 - block)
        oc = jnp.where(block < 4, 0, 1)
        src = l_ref.at[:, pl.ds(t * 512 + h * 256, 256)]
        dst = lbuf.at[h, zlo, y, zhi, pl.ds(c * 32, 32), :]
        mine = jnp.logical_and(ox == x, oc == c)
        needed = need(block, zlo, y)

        @pl.when(jnp.logical_and(needed, mine))
        def _():
            copy = pltpu.make_async_copy(src, dst, init_r.at[c, h])
            if act == "start":
                copy.start()

        @pl.when(jnp.logical_and(needed, jnp.logical_not(mine)))
        def _():
            copy = remote(src, dst, init_s.at[t, h], init_r.at[c, h], device(ox, y, z, oc))
            if act == "start":
                copy.start()
            else:
                copy.wait_send()

    for t in range(2):
        for h in range(2):
            init_copies(t, h, "start")

    mine_i = i2.at[pl.ds(c * 96, 96), :]
    copy_i = remote(i_ref, mine_i, i_s.at[0], i_r.at[0], sibling)
    copy_i.start()
    keep_i = pltpu.make_async_copy(i_ref, mine_i, i_s.at[1])
    keep_i.start()
    copy_e = remote(e_ref, eall.at[zlo], e_s, e_r, device(x, y, z_pair, c))
    copy_e.start()

    mine_needed = need(j, zlo, y)

    def wait_init(sc):
        @pl.when(mine_needed)
        def _():
            for h in range(2):
                slot = lbuf.at[h, zlo, y, zhi, sc * 32:(sc + 1) * 32, :]
                pltpu.make_async_copy(slot, slot, init_r.at[sc, h]).wait()

    def back(pos, s, d):
        return rem(pos + 8 - s, 8) if d == 0 else rem(pos + s, 8)

    def first(s, d, which, act):
        recv = act == "recv"
        step = s + 1 if recv else s
        sems = (a1_s, a1_r) if which == 0 else (b1_s, b1_r)
        if which == 0:
            o = back(y, step, d)
            ok = need(j, zlo, o)
            part = slice(0, 2) if s < 3 else slice(d, d + 1)
            ref = lbuf.at[part, zlo, o, zhi, 0:32, :]
            dev = y_side[d]
        else:
            o = back(z, step, d)
            ok = need(j, rem(o, 2), y)
            part = slice(0, 2) if s < 3 else slice(d, d + 1)
            ref = lbuf.at[part, rem(o, 2), y, div(o, 2), 32:64, :]
            dev = z_side[d]

        @pl.when(ok)
        def _():
            copy = remote(ref, ref, sems[0].at[d, s], sems[1].at[d, s], dev)
            if act == "start":
                copy.start()
            elif recv:
                copy.wait_recv()
            else:
                copy.wait_send()

    for which in range(2):
        wait_init(which)
        for d in range(2):
            first(0, d, which, "start")
    for s in range(1, 4):
        for which in range(2):
            for d in range(2):
                first(s - 1, d, which, "recv")
                first(s, d, which, "start")
    for which in range(2):
        for d in range(2):
            first(3, d, which, "recv")

    def second(s, d, which, piece, act):
        recv = act == "recv"
        step = s + 1 if recv else s
        if which == 0:
            o = back(z, step, d)
            zl = rem(o, 2)
            ok = zl * 4 + piece <= j
            ref = lbuf.at[d, zl, 2 * piece:2 * piece + 2, div(o, 2), 0:32, :]
            dev, ssem, rsem = z_side[d], a2_s.at[d, s, piece], a2_r.at[d, s, piece]
        else:
            o = back(y, step, d)
            ok = need(j, piece, o)
            ref = lbuf.at[d, piece, o, :, 32:64, :]
            dev, ssem, rsem = y_side[d], b2_s.at[d, s, piece], b2_r.at[d, s, piece]

        @pl.when(ok)
        def _():
            copy = remote(ref, ref, ssem, rsem, dev)
            if act == "start":
                copy.start()
            elif recv:
                copy.wait_recv()
            else:
                copy.wait_send()

    def pieces():
        for piece in range(4):
            for which in range(2):
                if which == 1 and piece > 1:
                    continue
                for d in range(2):
                    yield d, which, piece

    for d, which, piece in pieces():
        second(0, d, which, piece, "start")

    eall[zlo] = e_ref[...]
    copy_e.wait_recv()
    w = f_ref[0]
    for zl in range(2):
        e = eall[zl]
        fac = 2.0 * e / (e * e + w * w)
        for k in range(6):
            fcol[zl, k * 128:(k + 1) * 128, :] = jnp.broadcast_to(fac[k:k + 1, :], (128, 128)).T
    tacc[...] = jnp.zeros_like(tacc)
    r[...] = jnp.zeros_like(r)
    copy_i.wait_recv()
    keep_i.wait()

    @pl.loop(1, 7)
    def _(s):
        for d, which, piece in pieces():
            second(s - 1, d, which, piece, "recv")
            second(s, d, which, piece, "start")

    for d, which, piece in pieces():
        second(6, d, which, piece, "recv")

    @pl.loop(0, j + 1)
    def _(kt):
        left = i2[:, pl.ds(pl.multiple_of(kt * 512, 512), 512)]
        for h in range(2):
            right = lbuf[h, div(kt, 4), pl.ds(2 * rem(kt, 4), 2)].reshape(512, 256)
            tacc[h] += jnp.dot(left, right, preferred_element_type=F32)

    for h in range(2):
        tr[h, zlo, zhi] = tacc[h].astype(BF16)

    xr = jnp.where(z < 4, z, 7 - z)
    cr = jnp.where(z < 4, 0, 1)
    dist = rem(x + 4 - xr, 4)
    is_root = jnp.logical_and(dist == 0, c == cr)
    is_relay = jnp.logical_and(dist != 0, c == cr)

    def slot(buf, k, h):
        o = back(z, k, h)
        return buf.at[h, rem(o, 2), div(o, 2)]

    def z_copy(k, h):
        return remote(slot(tr, k, h), slot(tr, k, h), z_s.at[h, k], z_r.at[h, k], z_side[h])

    def z_wait(k, h):
        ref = slot(tr, k + 1, h)
        return remote(ref, ref, z_s.at[h, k], z_r.at[h, k], z_side[h]).wait_recv()

    def x_copy(src, k, h):
        return remote(slot(src, k, h), slot(tc, k, h), x_s.at[h, k], x_r.at[h, k],
                      x_next if h == 0 else x_prev)

    def c_copy(src, k, h):
        return remote(slot(src, k, h), slot(tc, k, h), c_s.at[h, k], x_r.at[h, k], sibling)

    def x_wait(k, h):
        pltpu.make_async_copy(slot(tc, k, h), slot(tc, k, h), x_r.at[h, k]).wait()

    def onward(h):
        return dist < 3 if h == 0 else dist > 1

    @pl.loop(0, 8 + LAG)
    def _(kk):
        for h in range(2):
            @pl.when(jnp.logical_and(kk >= 1, kk <= 7))
            def _():
                z_wait(kk - 1, h)

            @pl.when(kk <= 6)
            def _():
                z_copy(kk, h).start()

            @pl.when(jnp.logical_and(kk <= 7, is_root))
            def _():
                x_copy(tr, kk, h).start()
                c_copy(tr, kk, h).start()
                pltpu.make_async_copy(slot(tr, kk, h), slot(tc, kk, h), x_r.at[h, kk]).start()

        @pl.when(jnp.logical_and(kk >= LAG, is_relay))
        def _():
            for h in range(2):
                x_wait(kk - LAG, h)

                @pl.when(onward(h))
                def _():
                    x_copy(tc, kk - LAG, h).start()

                c_copy(tc, kk - LAG, h).start()

    @pl.when(jnp.logical_not(is_relay))
    def _():
        @pl.loop(0, 8)
        def _(k):
            for h in range(2):
                x_wait(k, h)

    @pl.loop(0, 4)
    def _(g):
        zl, zp = div(g, 2), 2 * rem(g, 2)
        fac = fcol[zl, pl.ds(pl.multiple_of(zp * 192, 384), 384), :]
        fac = jnp.concatenate([fac, fac], axis=1)
        for h in range(2):
            rows = tr[h, zl, pl.ds(zp, 2)].reshape(384, 256).astype(F32)
            rows = (fac * rows).astype(BF16)
            for v in range(2):
                cols = tc[v, zl, pl.ds(zp, 2)].reshape(384, 256)
                r[h * 256:(h + 1) * 256, v * 256:(v + 1) * 256] += lax.dot_general(
                    rows, cols, (((0,), (0,)), ((), ())), preferred_element_type=F32)

    def bufs(q, s):
        return (sb16, rb16) if s + 1 - q <= NARROW_TERMS else (sb32, rb32)

    def y_copy(d, q, s):
        sb, rb = bufs(q, s)
        return remote(sb.at[d, q, s], rb.at[d, q, s], y_s.at[d, q, s], y_r.at[d, q, s], y_side[d])

    def columns(d, q):
        v = d if q == 0 else 1 - d
        return slice(v * 256, (v + 1) * 256)

    for s in range(4):
        for q in range(2):
            if s < q:
                continue
            for d in range(2):
                dest = rem(y + 4 - s, 8) if d == 0 else rem(y + 4 + s, 8)
                total = r[pl.ds(pl.multiple_of(dest * 64, 64), 64), columns(d, q)]
                if s > q:
                    y_copy(d, q, s - 1).wait_recv()
                    total = total + bufs(q, s - 1)[1][d, q, s - 1].astype(F32)
                sb = bufs(q, s)[0]
                sb[d, q, s] = total.astype(sb.dtype)
                y_copy(d, q, s).start()
    for v in range(2):
        y_copy(v, 0, 3).wait_recv()
        y_copy(1 - v, 1, 3).wait_recv()
        res[:, v * 256:(v + 1) * 256] = (
            r[pl.ds(pl.multiple_of(y * 64, 64), 64), v * 256:(v + 1) * 256]
            + bufs(0, 3)[1][v, 0, 3].astype(F32)
            + bufs(1, 3)[1][1 - v, 1, 3].astype(F32))

    px, pz, pc = div(j, 2), rem(j, 2), zlo
    stays = jnp.logical_and(px == x, jnp.logical_and(pz == zlo, pc == c))
    out_copy = remote(res, out_ref, o_s, o_r, device(px, y, zhi * 2 + pz, pc))

    @pl.when(stays)
    def _():
        copy = pltpu.make_async_copy(res, out_ref, o_s)
        copy.start()
        copy.wait()

    @pl.when(jnp.logical_not(stays))
    def _():
        out_copy.start()

    for t in range(2):
        for h in range(2):
            init_copies(t, h, "wait")
    copy_i.wait_send()
    copy_e.wait_send()
    for which in range(2):
        for d in range(2):
            for s in range(4):
                first(s, d, which, "send")

    @pl.loop(0, 7)
    def _(s):
        for d, which, piece in pieces():
            second(s, d, which, piece, "send")
        for h in range(2):
            z_copy(s, h).wait_send()

    @pl.when(c == cr)
    def _():
        @pl.loop(0, 8)
        def _(k):
            for h in range(2):
                @pl.when(onward(h) | (dist == 0))
                def _():
                    x_copy(tc, k, h).wait_send()

                c_copy(tc, k, h).wait_send()

    for s in range(4):
        for q in range(2):
            if s < q:
                continue
            for d in range(2):
                y_copy(d, q, s).wait_send()

    @pl.when(jnp.logical_not(stays))
    def _():
        out_copy.wait()


def on_device(integrals, inverse_factor, energies, frequency):
    dma = pltpu.SemaphoreType.DMA
    vmem = pltpu.VMEM
    anywhere = pl.BlockSpec(memory_space=pl.ANY)
    return pl.pallas_call(
        kernel,
        out_shape=jax.ShapeDtypeStruct((64, 512), F32),
        in_specs=[
            anywhere,
            anywhere,
            pl.BlockSpec(memory_space=pltpu.VMEM),
            pl.BlockSpec(memory_space=pltpu.SMEM),
        ],
        out_specs=anywhere,
        scratch_shapes=[
            vmem((2, 2, 8, 4, 64, 256), BF16),
            vmem((192, 4096), BF16),
            vmem((2, 192, 256), F32),
            vmem((2, 2, 4, 192, 256), BF16),
            vmem((2, 2, 4, 192, 256), BF16),
            vmem((2, 6, 128), F32),
            vmem((2, 768, 128), F32),
            vmem((512, 512), F32),
            vmem((2, 2, 4, 64, 256), BF16),
            vmem((2, 2, 4, 64, 256), F32),
            vmem((2, 2, 4, 64, 256), BF16),
            vmem((2, 2, 4, 64, 256), F32),
            vmem((64, 512), F32),
            dma((2, 2)), dma((2, 2)), dma((2,)), dma((1,)), dma, dma,
            dma((2, 4)), dma((2, 4)), dma((2, 4)), dma((2, 4)),
            dma((2, 7, 4)), dma((2, 7, 4)), dma((2, 7, 2)), dma((2, 7, 2)),
            dma((2, 7)), dma((2, 7)), dma((2, 8)), dma((2, 8)), dma((2, 8)),
            dma((2, 2, 4)), dma((2, 2, 4)), dma, dma,
        ],
        compiler_params=pltpu.CompilerParams(
            collective_id=0, has_side_effects=True, vmem_limit_bytes=40 * 1024 * 1024),
    )(integrals, inverse_factor.T, energies.reshape(6, 128), frequency)


def solution(mesh):
    return jax.shard_map(
        on_device,
        mesh=mesh,
        in_specs=(P(("pair", "col"), None), P("row", ("pair", "col")), P("pair"), P()),
        out_specs=P(("row", "pair"), "col"),
        check_vma=False,
    )
```

time: 452 us -> 218 us (0.48)
  the two profiles are of different devices: /device:TPU:4 before, /device:TPU:3 now
where the time goes in v1:
time: 218 us
  Pallas kernels  215 us (99%)
  local copies, waits for them, and re-layouts  2.65 us (1%)
    pallas_call x1, Pallas kernels, on_device(): pl.pallas_call(kernel, out_shape=jax.ShapeDtypeStruct((64, 512), F32), in...  215 us

profile of v1, /device:TPU:3, one launch (start us, length us, event | category | flops | bytes accessed | tf_op | source)
XLA Modules:
  0.0 218.0 jit_solution(4081688334345067575)
XLA Ops:
  0.0 0.0 copy-start.2
  0.7 0.0 copy-done.2
  0.7 0.0 copy-start
  0.7 1.1 copy-done
  1.8 0.0 copy-start.1
  1.8 0.8 copy-done.1
  2.7 214.7 %shard_map.46 = f32[64,512]{1,0:T(8,128)S(1)} custom-call(bf16[96,4096]{1,0:T(8,128)(2,1)S(1)} %copy-done, bf16[32,1024]{1,0:T(8,128)(2,1)S(1)} %bitcast.2, f32[6,128]{1,0:T(8,128)S(1)} %bitcast.3, f32[1]{0:T(128)S(6)} %copy.6.f_ref), custom_call_target="tpu_custom_call" | custom-call | tf_op jit(solution)/shard_map/pallas_call | solution.py:388
  217.4 0.7 copy.7
Async XLA Ops:
  0.0 0.7 copy-start.2
  0.7 1.1 copy-start
  1.8 0.8 copy-start.1

commit v2 on v0

v2 whole, which is shorter than its diff:
```python
import jax
import jax.numpy as jnp
from jax import lax
from jax.experimental import pallas as pl
from jax.experimental.pallas import tpu as pltpu
from jax.sharding import PartitionSpec as P

MESH = pl.DeviceIdType.MESH
F32, BF16 = jnp.float32, jnp.bfloat16
FAR_FIRST = (4, 3, 5, 2, 6, 1, 7)


def rem(a, b):
    return lax.rem(a, jnp.int32(b))


def div(a, b):
    return lax.div(a, jnp.int32(b))


def device(x, y, z, c):
    return {"pair": rem(z, 2) * 8 + y, "row": x, "col": div(z, 2) * 2 + c}


def kernel(
    i_ref, l_ref, e_ref, f_ref, out_ref,
    lbuf, i2, tacc, tr, tc, eall, fcol, r, sb, rb,
    init_s, init_r, i_s, i_r, e_s, e_r,
    near_s, near_r, far_s, far_r,
    z_s, z_r, x_s, c_s, x_r, o_s, o_r,
):
    pair, x, col = lax.axis_index("pair"), lax.axis_index("row"), lax.axis_index("col")
    zlo, y = div(pair, 8), rem(pair, 8)
    zhi, c = div(col, 2), rem(col, 2)
    z = zhi * 2 + zlo
    j = jnp.where(c == 0, x, 7 - x)
    sibling = device(x, y, z, 1 - c)
    x_side = (device(rem(x + 1, 4), y, z, c), device(rem(x + 3, 4), y, z, c))
    y_side = (device(x, rem(y + 1, 8), z, c), device(x, rem(y + 7, 8), z, c))
    z_side = (device(x, y, rem(z + 1, 8), c), device(x, y, rem(z + 7, 8), c))
    z_pair = zhi * 2 + 1 - zlo
    px, pz, pc = div(j, 2), rem(j, 2), zlo
    stays = jnp.logical_and(px == x, jnp.logical_and(pz == zlo, pc == c))
    here = 2 * x + zlo
    sx, sz = jnp.where(here < 4, here, 7 - here), c
    sc = jnp.where(here < 4, 0, 1)

    def remote(src, dst, ssem, rsem, dev):
        return pltpu.make_async_remote_copy(
            src_ref=src, dst_ref=dst, send_sem=ssem, recv_sem=rsem,
            device_id=dev, device_id_type=MESH)

    keep_i = pltpu.make_async_copy(i_ref, i2.at[pl.ds(c * 96, 96), :], i_s.at[1])
    keep_i.start()

    barrier = pltpu.get_barrier_semaphore()

    def hello(dev):
        pl.semaphore_signal(barrier, inc=1, device_id_type=MESH, device_id=dev)

    for k in FAR_FIRST:
        hello(device(px, rem(y + k, 8), zhi * 2 + pz, pc))
        hello(device(sx, rem(y + k, 8), zhi * 2 + sz, sc))
        hello(device(x, rem(y + k, 8), z, c))
    for k in range(1, 4):
        for zl in range(2):
            hello(device(x, y, rem(zhi + k, 4) * 2 + zl, c))
    for k in range(1, 16):
        dx, dz, dc = k // 4, (k // 2) % 2, k % 2
        hello(device(rem(x + dx, 4), y, zhi * 2 + rem(zlo + dz, 2), rem(c + dc, 2)))
    pl.semaphore_wait(barrier, 21 + 6 + 15)

    def need(zl, yy):
        return zl * 4 + div(yy, 2) <= j

    def init_copies(t, act):
        block = 2 * x + t
        ox = jnp.where(block < 4, block, 7 - block)
        oc = jnp.where(block < 4, 0, 1)
        src = l_ref.at[:, pl.ds(t * 512, 512)]
        dst = lbuf.at[zlo, y, zhi, pl.ds(c * 32, 32), :]
        mine = jnp.logical_and(ox == x, oc == c)
        needed = zlo * 4 + div(y, 2) <= block

        @pl.when(jnp.logical_and(needed, mine))
        def _():
            if act == "start":
                pltpu.make_async_copy(src, dst, init_r.at[c]).start()

        @pl.when(jnp.logical_and(needed, jnp.logical_not(mine)))
        def _():
            copy = remote(src, dst, init_s.at[t], init_r.at[c], device(ox, y, z, oc))
            if act == "start":
                copy.start()
            else:
                copy.wait_send()

    for t in range(2):
        init_copies(t, "start")
    copy_e = remote(e_ref, eall.at[zlo], e_s, e_r, device(x, y, z_pair, c))
    copy_e.start()

    mine_needed = need(zlo, y)

    def block(which, zl, yy, zh):
        return lbuf.at[zl, yy, zh, which * 32:which * 32 + 32, :]

    def near(which, k):
        ref = block(which, zlo, y, zhi)
        dev = device(x, rem(y + k, 8), z, c) if which == 0 else device(x, y, rem(z + k, 8), c)
        return remote(ref, ref, near_s.at[which, k], near_r.at[which, k], dev)

    def near_wait(which, k):
        if which == 0:
            ref, ok = block(0, zlo, rem(y + 8 - k, 8), zhi), need(zlo, rem(y + 8 - k, 8))
        else:
            o = rem(z + 8 - k, 8)
            ref, ok = block(1, rem(o, 2), y, div(o, 2)), need(rem(o, 2), y)

        @pl.when(jnp.logical_and(ok, k != 0))
        def _():
            pltpu.make_async_copy(ref, ref, near_r.at[which, k]).wait()

    @pl.when(mine_needed)
    def _():
        for which in range(2):
            ref = block(which, zlo, y, zhi)
            pltpu.make_async_copy(ref, ref, init_r.at[which]).wait()
            for k in FAR_FIRST:
                near(which, k).start()

    copy_i = remote(i_ref, i2.at[pl.ds(c * 96, 96), :], i_s.at[0], i_r.at[0], sibling)
    copy_i.start()

    def back(pos, s, d):
        return rem(pos + 8 - s, 8) if d == 0 else rem(pos + s, 8)

    def far(s, d, which, piece, act):
        step = s + 1 if act == "recv" else s
        if which == 0:
            o = back(z, step, d)
            ok = rem(o, 2) * 4 + piece <= j
            ref = lbuf.at[rem(o, 2), 2 * piece:2 * piece + 2, div(o, 2), 0:32, :]
            dev = z_side[d]
        else:
            o = back(y, step, d)
            zl, half = piece // 2, piece % 2
            ok = need(zl, o)
            ref = lbuf.at[zl, o, 2 * half:2 * half + 2, 32:64, :]
            dev = y_side[d]

        @pl.when(ok)
        def _():
            copy = remote(
                ref, ref, far_s.at[which, d, s, piece], far_r.at[which, d, s, piece], dev)
            if act == "start":
                copy.start()
            elif act == "recv":
                copy.wait_recv()
            else:
                copy.wait_send()

    for piece in range(4):
        for k in range(2):
            near_wait(0, rem(y + 8 - (2 * piece + k), 8))
        for d in range(2):
            far(0, d, 0, piece, "start")
        zl, half = piece // 2, piece % 2
        for k in range(2):
            near_wait(1, rem(z + 8 - (4 * half + 2 * k + zl), 8))
        for d in range(2):
            far(0, d, 1, piece, "start")

    eall[zlo] = e_ref[...]
    copy_e.wait_recv()
    w = f_ref[0]
    for zl in range(2):
        e = eall[zl]
        fac = 2.0 * e / (e * e + w * w)
        for k in range(6):
            fcol[zl, k * 128:(k + 1) * 128, :] = jnp.broadcast_to(fac[k:k + 1, :], (128, 128)).T
    tacc[...] = jnp.zeros_like(tacc)
    r[...] = jnp.zeros_like(r)

    for s in range(1, 4):
        for piece in range(4):
            for which in range(2):
                for d in range(2):
                    far(s - 1, d, which, piece, "recv")
                    if s < 3 or piece % 2 == d:
                        far(s, d, which, piece, "start")
    copy_i.wait_recv()
    keep_i.wait()
    for piece in range(4):
        for which in range(2):
            far(3, piece % 2, which, piece, "recv")

    @pl.loop(0, j + 1)
    def _(kt):
        left = i2[:, pl.ds(pl.multiple_of(kt * 512, 512), 512)]
        right = lbuf[div(kt, 4), pl.ds(2 * rem(kt, 4), 2)].reshape(512, 512)
        tacc[...] += jnp.dot(left, right, preferred_element_type=F32)

    tr[zlo, zhi] = tacc[...].astype(BF16)

    xr = jnp.where(z < 4, z, 7 - z)
    cr = jnp.where(z < 4, 0, 1)
    dist = rem(x + 4 - xr, 4)
    is_root = jnp.logical_and(dist == 0, c == cr)

    def part(buf, o, p):
        return buf.at[rem(o, 2), div(o, 2), p * 96:(p + 1) * 96, :]

    def z_copy(s, d, p):
        ref = part(tr, back(z, s, d), p)
        return remote(ref, ref, z_s.at[d, s, p], z_r.at[d, s, p], z_side[d])

    def z_wait(s, d, p):
        ref = part(tr, back(z, s + 1, d), p)
        remote(ref, ref, z_s.at[d, s, p], z_r.at[d, s, p], z_side[d]).wait_recv()

    def arrivals(s):
        if s == 0:
            return [(p, z, p) for p in range(2)]
        if s == 4:
            return [(14 + d, back(z, 4, d), d) for d in range(2)]
        return [(4 * s - 2 + 2 * p + d, back(z, s, d), p) for p in range(2) for d in range(2)]

    def root_send(n, o, p):
        for k in range(2):
            remote(part(tr, o, p), part(tc, o, p), x_s.at[k, n], x_r.at[n], x_side[k]).start()
        remote(part(tr, o, p), part(tc, o, p), c_s.at[n], x_r.at[n], sibling).start()
        pltpu.make_async_copy(part(tr, o, p), part(tc, o, p), x_r.at[n]).start()

    def x_wait(n, o, p):
        pltpu.make_async_copy(part(tc, o, p), part(tc, o, p), x_r.at[n]).wait()

    def relay(n, o, p):
        x_wait(n, o, p)

        @pl.when(dist == (1 if p == 0 else 3))
        def _():
            remote(part(tc, o, p), part(tc, o, p), x_s.at[p, n], x_r.at[n], x_side[p]).start()

        remote(part(tc, o, p), part(tc, o, p), c_s.at[n], x_r.at[n], sibling).start()

    for p in range(2):
        for d in range(2):
            z_copy(0, d, p).start()

    for s in range(7):
        if s == 0:
            @pl.when(is_root)
            def _():
                for a in arrivals(0):
                    root_send(*a)
        elif s < 5:
            for n, o, p in arrivals(s):
                d = (n - (4 * s - 2)) % 2 if s < 4 else p
                z_wait(s - 1, d, p)
                if s < 3 or (s == 3 and p == d):
                    z_copy(s, d, p).start()

                @pl.when(is_root)
                def _():
                    root_send(n, o, p)
        if 1 <= s <= 5:
            @pl.when(jnp.logical_and(c == cr, rem(dist, 2) == 1))
            def _():
                for a in arrivals(s - 1):
                    relay(*a)
        if 2 <= s:
            @pl.when(jnp.logical_and(c == cr, dist == 2))
            def _():
                for a in arrivals(s - 2):
                    relay(*a)

    @pl.when(jnp.logical_or(c != cr, is_root))
    def _():
        for s in range(5):
            for a in arrivals(s):
                x_wait(*a)

    @pl.loop(0, 4)
    def _(g):
        zl, zp = div(g, 2), 2 * rem(g, 2)
        fac = fcol[zl, pl.ds(pl.multiple_of(zp * 192, 384), 384), :]
        fac = jnp.concatenate([fac] * 4, axis=1)
        rows = tr[zl, pl.ds(zp, 2)].reshape(384, 512).astype(F32)
        rows = (fac * rows).astype(BF16)
        cols = tc[zl, pl.ds(zp, 2)].reshape(384, 512)
        r[...] += lax.dot_general(
            rows, cols, (((0,), (0,)), ((), ())), preferred_element_type=F32)

    sb[...] = r[...].reshape(8, 64, 512).astype(BF16)

    def out_copy(k):
        to = rem(y + k, 8)
        return remote(
            sb.at[to], rb.at[k], o_s.at[k], o_r.at[k], device(px, to, zhi * 2 + pz, pc))

    for k in FAR_FIRST:
        out_copy(k).start()

    @pl.when(stays)
    def _():
        pltpu.make_async_copy(sb.at[y], rb.at[0], o_r.at[0]).start()

    @pl.when(jnp.logical_not(stays))
    def _():
        out_copy(0).start()

    pltpu.make_async_copy(rb.at[0], rb.at[0], o_r.at[0]).wait()
    total = rb[0].astype(F32)
    for k in (1, 7, 2, 6, 3, 5, 4):
        out_copy(k).wait_recv()
        total = total + rb[k].astype(F32)
    out_ref[...] = total

    for t in range(2):
        init_copies(t, "wait")
    copy_i.wait_send()
    copy_e.wait_send()

    @pl.when(mine_needed)
    def _():
        for which in range(2):
            for k in FAR_FIRST:
                near(which, k).wait_send()

    for s in range(4):
        for piece in range(4):
            for which in range(2):
                for d in range(2):
                    if s < 3 or piece % 2 == d:
                        far(s, d, which, piece, "send")
    for s in range(4):
        for p in range(2):
            for d in range(2):
                if s < 3 or p == d:
                    z_copy(s, d, p).wait_send()

    for s in range(5):
        for n, o, p in arrivals(s):
            ref = part(tc, o, p)
            for k in range(2):
                @pl.when(jnp.logical_or(
                    is_root,
                    jnp.logical_and(c == cr, dist == (1 if k == 0 else 3)) if k == p else False))
                def _():
                    remote(ref, ref, x_s.at[k, n], x_r.at[n], x_side[k]).wait_send()

            @pl.when(c == cr)
            def _():
                remote(ref, ref, c_s.at[n], x_r.at[n], sibling).wait_send()

    for k in FAR_FIRST:
        out_copy(k).wait_send()

    @pl.when(jnp.logical_not(stays))
    def _():
        out_copy(0).wait_send()


def on_device(integrals, inverse_factor, energies, frequency):
    dma = pltpu.SemaphoreType.DMA
    vmem = pltpu.VMEM
    anywhere = pl.BlockSpec(memory_space=pl.ANY)
    return pl.pallas_call(
        kernel,
        out_shape=jax.ShapeDtypeStruct((64, 512), F32),
        in_specs=[
            anywhere,
            anywhere,
            pl.BlockSpec(memory_space=pltpu.VMEM),
            pl.BlockSpec(memory_space=pltpu.SMEM),
        ],
        out_specs=pl.BlockSpec(memory_space=pltpu.VMEM),
        scratch_shapes=[
            vmem((2, 8, 4, 64, 512), BF16),
            vmem((192, 4096), BF16),
            vmem((192, 512), F32),
            vmem((2, 4, 192, 512), BF16),
            vmem((2, 4, 192, 512), BF16),
            vmem((2, 6, 128), F32),
            vmem((2, 768, 128), F32),
            vmem((512, 512), F32),
            vmem((8, 64, 512), BF16),
            vmem((8, 64, 512), BF16),
            dma((2,)), dma((2,)), dma((2,)), dma((1,)), dma, dma,
            dma((2, 8)), dma((2, 8)), dma((2, 2, 4, 4)), dma((2, 2, 4, 4)),
            dma((2, 4, 2)), dma((2, 4, 2)), dma((2, 16)), dma((16,)), dma((16,)),
            dma((8,)), dma((8,)),
        ],
        compiler_params=pltpu.CompilerParams(
            collective_id=0, has_side_effects=True, vmem_limit_bytes=60 * 1024 * 1024),
    )(integrals, inverse_factor.T, energies.reshape(6, 128), frequency)


def solution(mesh):
    return jax.shard_map(
        on_device,
        mesh=mesh,
        in_specs=(P(("pair", "col"), None), P("row", ("pair", "col")), P("pair"), P()),
        out_specs=P(("row", "pair"), "col"),
        check_vma=False,
    )
```

time: 452 us -> 94 us (0.21)
  the two profiles are of different devices: /device:TPU:4 before, /device:TPU:5 now
where the time goes in v2:
time: 94 us; the launch traced here: 93.8 us
  Pallas kernels  91.5 us (97%)
  local copies, waits for them, and re-layouts  1.57 us (2%)
    pallas_call x1, Pallas kernels, on_device(): pl.pallas_call(kernel, out_shape=jax.ShapeDtypeStruct((64, 512), F32), in...  91.5 us

profile of v2, /device:TPU:5, one launch (start us, length us, event | category | flops | bytes accessed | tf_op | source)
XLA Modules:
  0.0 93.8 jit_solution(8897863719929512657)
XLA Ops:
  0.7 91.5 %shard_map.46 = f32[64,512]{1,0:T(8,128)} custom-call(bf16[96,4096]{1,0:T(8,128)(2,1)} %i_ref.1, bf16[32,1024]{1,0:T(8,128)(2,1)} %bitcast.2, f32[6,128]{1,0:T(8,128)} %bitcast.3, f32[1]{0:T(128)S(6)} %copy.6.f_ref), custom_call_target="tpu_custom_call" | custom-call | tf_op jit(solution)/shard_map/pallas_call | solution.py:369
  92.2 1.6 %copy.7 = f32[64,512]{1,0:T(8,128)} copy(f32[64,512]{1,0:T(8,128)} %shard_map.46) | data formatting | bytes 262144

commit v3 on v2

v3 whole, which is shorter than its diff:
```python
import jax
import jax.numpy as jnp
from jax import lax
from jax.experimental import pallas as pl
from jax.experimental.pallas import tpu as pltpu
from jax.sharding import PartitionSpec as P

MESH = pl.DeviceIdType.MESH
F32, BF16 = jnp.float32, jnp.bfloat16
FAR_FIRST = (4, 3, 5, 2, 6, 1, 7)


def rem(a, b):
    return lax.rem(a, jnp.int32(b))


def div(a, b):
    return lax.div(a, jnp.int32(b))


def device(x, y, z, c):
    return {"pair": rem(z, 2) * 8 + y, "row": x, "col": div(z, 2) * 2 + c}


def kernel(
    i_ref, l_ref, e_ref, f_ref, out_ref,
    lbuf, i2, tacc, tr, tc, eall, fcol, r, sb, rb, mid, half_mid, sb2,
    i_s, i_r, e_s, e_r,
    near_s, near_r, far_s, far_r,
    z_s, z_r, x_s, x2_s, c_s, x_r, m_s, m_r, h_s, h_r, o_s, o_r,
):
    pair, x, col = lax.axis_index("pair"), lax.axis_index("row"), lax.axis_index("col")
    zlo, y = div(pair, 8), rem(pair, 8)
    zhi, c = div(col, 2), rem(col, 2)
    z = zhi * 2 + zlo
    low = jnp.where(x == 3, 0, jnp.where(x == 0, 1, jnp.where(x == 2, 2, 3)))
    j = jnp.where(c == 0, low, 7 - low)

    def owner(block):
        low = jnp.where(block < 4, block, 7 - block)
        ox = jnp.where(low == 0, 3, jnp.where(low == 1, 0, jnp.where(low == 2, 2, 1)))
        return ox, jnp.where(block < 4, 0, 1)

    sibling = device(x, y, z, 1 - c)
    x_side = (device(rem(x + 1, 4), y, z, c), device(rem(x + 3, 4), y, z, c))
    y_side = (device(x, rem(y + 1, 8), z, c), device(x, rem(y + 7, 8), z, c))
    z_side = (device(x, y, rem(z + 1, 8), c), device(x, y, rem(z + 7, 8), c))
    z_pair = zhi * 2 + 1 - zlo
    px, pz, pc = div(j, 2), rem(j, 2), zlo
    stays = jnp.logical_and(px == x, jnp.logical_and(pz == zlo, pc == c))
    (sx, sc), sz = owner(2 * x + zlo), c

    def remote(src, dst, ssem, rsem, dev):
        return pltpu.make_async_remote_copy(
            src_ref=src, dst_ref=dst, send_sem=ssem, recv_sem=rsem,
            device_id=dev, device_id_type=MESH)

    keep_i = pltpu.make_async_copy(i_ref, i2.at[pl.ds(c * 96, 96), :], i_s.at[1])
    keep_i.start()

    barrier = pltpu.get_barrier_semaphore()

    def hello(dev):
        pl.semaphore_signal(barrier, inc=1, device_id_type=MESH, device_id=dev)

    def factor_target(t, k, half):
        ox, oc = owner(2 * x + t)
        across = z_pair if half else z
        return device(
            ox, rem(y + jnp.where(c == 0, k, 0), 8),
            jnp.where(c == 0, across, rem(z + k, 8)), oc)

    def factor_source(which, k, half):
        if which == 0:
            return device(div(j, 2), rem(y + 8 - k, 8), z_pair if half else z, 0)
        return device(div(j, 2), y, rem(z + 8 - k, 8), 1)

    def own_block(t):
        ox, oc = owner(2 * x + t)
        return jnp.logical_and(ox == x, oc == c)

    own_any = jnp.logical_or(own_block(0), own_block(1))
    for k in FAR_FIRST:
        for t in range(2):
            hello(factor_target(t, k, 0))
            hello(factor_source(t, k, 0))

            @pl.when(c == 0)
            def _():
                hello(factor_target(t, k, 1))

        hello(factor_source(0, k, 1))
    for t in range(2):
        @pl.when(jnp.logical_not(own_block(t)))
        def _():
            hello(factor_target(t, 0, 0))

        @pl.when(jnp.logical_or(div(j, 2) != x, c != t))
        def _():
            hello(factor_source(t, 0, 0))
    for k in (6, 2, 7, 1):
        hello(device(px, rem(y + k, 8), zhi * 2 + pz, pc))
        hello(device(sx, rem(y + k, 8), zhi * 2 + sz, sc))
        hello(device(x, rem(y + k, 8), z, c))
    hello(device(x, y, jnp.where(zlo == 1, rem(z + 1, 8), rem(z + 7, 8)), c))
    for k in range(1, 16):
        dx, dz, dc = k // 4, (k // 2) % 2, k % 2
        hello(device(rem(x + dx, 4), y, zhi * 2 + rem(zlo + dz, 2), rem(c + dc, 2)))
    pl.semaphore_wait(
        barrier, 39 + 12 + 1 + 15 + jnp.where(c == 0, 14, 0) - jnp.where(own_any, 2, 0))

    def need(zl, yy):
        return zl * 4 + div(yy, 2) <= j

    def factor_rows(t, k, half, act):
        src = l_ref.at[half * 16:half * 16 + 16, pl.ds(t * 512, 512)]
        dst = lbuf.at[zlo, y, zhi, pl.ds(c * 32 + half * 16, 16), :]
        needed = zlo * 4 + div(y, 2) <= 2 * x + t
        if k == 0:
            mine = jnp.logical_and(own_block(t), jnp.logical_or(half == 0, c == 1))

            @pl.when(jnp.logical_and(needed, mine))
            def _():
                if act == "start":
                    pltpu.make_async_copy(src, dst, near_r.at[c, 0, half]).start()

            needed = jnp.logical_and(needed, jnp.logical_not(mine))

        @pl.when(needed)
        def _():
            copy = remote(
                src, dst, near_s.at[t, k, half], near_r.at[c, k, half], factor_target(t, k, half))
            if act == "start":
                copy.start()
            else:
                copy.wait_send()

    for k in (*FAR_FIRST, 0):
        for t in range(2):
            for half in range(2):
                factor_rows(t, k, half, "start")
    copy_e = remote(e_ref, eall.at[zlo], e_s, e_r, device(x, y, z_pair, c))
    copy_e.start()

    def near_wait(zl, yy, zh, first, k, which, half):
        ref = lbuf.at[zl, yy, zh, pl.ds(first, 16), :]

        @pl.when(need(zl, yy))
        def _():
            pltpu.make_async_copy(ref, ref, near_r.at[which, k, half]).wait()

    def near_wait_y(zl, yy):
        half = jnp.where(zlo == zl, 0, 1)
        near_wait(zl, yy, zhi, half * 16, rem(y + 8 - yy, 8), 0, half)

    def near_wait_z(zl, zh):
        for half in range(2):
            near_wait(zl, y, zh, 32 + 16 * half, rem(z + 8 - (2 * zh + zl), 8), 1, half)

    copy_i = remote(i_ref, i2.at[pl.ds(c * 96, 96), :], i_s.at[0], i_r.at[0], sibling)
    copy_i.start()

    def back(pos, s, d):
        return rem(pos + 8 - s, 8) if d == 0 else rem(pos + s, 8)

    def far(s, d, which, piece, act):
        step = s + 1 if act == "recv" else s
        if which == 0:
            o = back(z, step, d)
            zl, u = piece // 4, piece % 4
            ok = piece <= j
            first = jnp.where(rem(o, 2) == zl, 0, 16)
            ref = lbuf.at[zl, 2 * u:2 * u + 2, div(o, 2), pl.ds(first, 16), :]
            dev = z_side[d]
        else:
            o = back(y, step, d)
            zl, half = piece // 2, piece % 2
            ok = need(zl, o)
            ref = lbuf.at[zl, o, 2 * half:2 * half + 2, 32:64, :]
            dev = y_side[d]

        @pl.when(ok)
        def _():
            copy = remote(
                ref, ref, far_s.at[which, d, s, piece], far_r.at[which, d, s, piece], dev)
            if act == "start":
                copy.start()
            elif act == "recv":
                copy.wait_recv()
            else:
                copy.wait_send()

    def pieces():
        for u in range(4):
            for which, piece in ((0, u), (0, u + 4), (1, u)):
                yield which, piece

    for which, piece in pieces():
        if which == 0:
            for k in range(2):
                near_wait_y(piece // 4, 2 * (piece % 4) + k)
        else:
            for k in range(2):
                near_wait_z(piece // 2, 2 * (piece % 2) + k)
        for d in range(2):
            far(0, d, which, piece, "start")

    eall[zlo] = e_ref[...]
    copy_e.wait_recv()
    w = f_ref[0]
    for zl in range(2):
        e = eall[zl]
        fac = 2.0 * e / (e * e + w * w)
        for k in range(6):
            fcol[zl, k * 128:(k + 1) * 128, :] = jnp.broadcast_to(fac[k:k + 1, :], (128, 128)).T
    tacc[...] = jnp.zeros_like(tacc)
    r[...] = jnp.zeros_like(r)

    for s in range(1, 4):
        for which, piece in pieces():
            for d in range(2):
                far(s - 1, d, which, piece, "recv")
                if s < 3 or piece % 2 == d:
                    far(s, d, which, piece, "start")
    copy_i.wait_recv()
    keep_i.wait()
    for which, piece in pieces():
        far(3, piece % 2, which, piece, "recv")

    @pl.loop(0, j + 1)
    def _(kt):
        left = i2[:, pl.ds(pl.multiple_of(kt * 512, 512), 512)]
        right = lbuf[div(kt, 4), pl.ds(2 * rem(kt, 4), 2)].reshape(512, 512)
        tacc[...] += jnp.dot(left, right, preferred_element_type=F32)

    tr[zlo, zhi] = tacc[...].astype(BF16)

    xr, cr = owner(z)
    dist = rem(x + 4 - xr, 4)
    is_root = jnp.logical_and(dist == 0, c == cr)

    def part(buf, o, p):
        return buf.at[rem(o, 2), div(o, 2), p * 96:(p + 1) * 96, :]

    def small(o, q):
        return tr.at[rem(o, 2), div(o, 2), q * 48:(q + 1) * 48, :]

    def z_copy(s, d, q):
        ref = small(back(z, s, d), q)
        return remote(ref, ref, z_s.at[d, s, q], z_r.at[d, s, q], z_side[d])

    def z_wait(s, d, q):
        ref = small(back(z, s + 1, d), q)
        remote(ref, ref, z_s.at[d, s, q], z_r.at[d, s, q], z_side[d]).wait_recv()

    def arrivals(s):
        if s == 0:
            return [(p, z, p) for p in range(2)]
        if s == 4:
            return [(14 + d, back(z, 4, d), d) for d in range(2)]
        return [(4 * s - 2 + 2 * p + d, back(z, s, d), p) for p in range(2) for d in range(2)]

    def root_send(n, o, p):
        if n >= 14:
            remote(part(tr, o, p), part(tc, o, p), x2_s.at[p], x_r.at[n],
                   device(rem(x + 2, 4), y, z, c)).start()
        for k in range(2):
            remote(part(tr, o, p), part(tc, o, p), x_s.at[k, n], x_r.at[n], x_side[k]).start()
        remote(part(tr, o, p), part(tc, o, p), c_s.at[n], x_r.at[n], sibling).start()
        pltpu.make_async_copy(part(tr, o, p), part(tc, o, p), x_r.at[n]).start()

    def x_wait(n, o, p):
        pltpu.make_async_copy(part(tc, o, p), part(tc, o, p), x_r.at[n]).wait()

    def relay(n, o, p):
        x_wait(n, o, p)
        if n < 14:
            @pl.when(dist == (1 if p == 0 else 3))
            def _():
                remote(part(tc, o, p), part(tc, o, p), x_s.at[p, n], x_r.at[n], x_side[p]).start()

        remote(part(tc, o, p), part(tc, o, p), c_s.at[n], x_r.at[n], sibling).start()

    def add_chunks(s):
        for o in (z,) if s == 0 else (back(z, s, 0), back(z, s, 1))[:1 if s == 4 else 2]:
            zl, zh = rem(o, 2), div(o, 2)
            fac = fcol[zl, pl.ds(pl.multiple_of(zh * 192, 64), 192), :]
            fac = jnp.concatenate([fac] * 4, axis=1)
            rows = (fac * tr[zl, zh].astype(F32)).astype(BF16)
            product = lax.dot_general(
                rows, tc[zl, zh], (((0,), (0,)), ((), ())), preferred_element_type=F32)
            r[...] += product

    def settle(s):
        @pl.when(jnp.logical_or(c != cr, is_root))
        def _():
            for a in arrivals(s):
                x_wait(*a)

        add_chunks(s)

    for q in range(4):
        for d in range(2):
            z_copy(0, d, q).start()

    copy_i.wait_send()
    copy_e.wait_send()
    for k in range(8):
        for t in range(2):
            for half in range(2):
                factor_rows(t, k, half, "wait")
    for s in range(4):
        for which, piece in pieces():
            for d in range(2):
                if s < 3 or piece % 2 == d:
                    far(s, d, which, piece, "send")

    for s in range(7):
        if s == 0:
            @pl.when(is_root)
            def _():
                for a in arrivals(0):
                    root_send(*a)
        elif s < 5:
            for n, o, p in arrivals(s):
                d = (n - (4 * s - 2)) % 2 if s < 4 else p
                for q in (2 * p, 2 * p + 1):
                    z_wait(s - 1, d, q)
                    if s < 3 or (s == 3 and p == d):
                        z_copy(s, d, q).start()

                @pl.when(is_root)
                def _():
                    root_send(n, o, p)
        if 1 <= s <= 5:
            @pl.when(jnp.logical_and(c == cr, rem(dist, 2) == 1))
            def _():
                for a in arrivals(s - 1):
                    relay(*a)
        if 2 <= s:
            @pl.when(jnp.logical_and(c == cr, dist == 2))
            def _():
                for a in arrivals(s - 2):
                    relay(*a)
        if s == 4:
            settle(0)
            settle(1)
        if s == 5:
            settle(2)
    settle(3)
    settle(4)

    def rows_of(k):
        return r[pl.ds(pl.multiple_of(rem(y + k, 8) * 64, 64), 64), :]

    def mid_copy(d):
        return remote(sb.at[3 if d == 0 else 5], mid.at[d], m_s.at[d], m_r.at[d], y_side[d])

    def half_copy(d):
        return remote(
            sb.at[4, :, d * 256:(d + 1) * 256], half_mid.at[d], h_s.at[d], h_r.at[d],
            device(x, rem(y + (2 if d == 0 else 6), 8), z, c))

    def out_copy(k):
        src = sb2.at[0 if k == 2 else 1] if k in (2, 6) else sb.at[k]
        return remote(
            src, rb.at[k], o_s.at[k], o_r.at[k], device(px, rem(y + k, 8), zhi * 2 + pz, pc))

    sb[4] = rows_of(4).astype(BF16)
    for d in range(2):
        half_copy(d).start()
    for d in range(2):
        sb[3 if d == 0 else 5] = rows_of(3 if d == 0 else 5).astype(BF16)
        mid_copy(d).start()
    for k in (1, 7):
        sb[k] = rows_of(k).astype(BF16)
        out_copy(k).start()
    sb[0] = rows_of(0).astype(BF16)

    @pl.when(stays)
    def _():
        pltpu.make_async_copy(sb.at[0], rb.at[0], o_r.at[0]).start()

    @pl.when(jnp.logical_not(stays))
    def _():
        out_copy(0).start()

    for s in range(4):
        for q in range(4):
            for d in range(2):
                if s < 3 or q // 2 == d:
                    z_copy(s, d, q).wait_send()
    for s in range(5):
        for n, o, p in arrivals(s):
            ref = part(tc, o, p)
            for k in range(2):
                relays = jnp.logical_and(c == cr, dist == (1 if k == 0 else 3))

                @pl.when(jnp.logical_or(is_root, relays) if k == p and n < 14 else is_root)
                def _():
                    remote(ref, ref, x_s.at[k, n], x_r.at[n], x_side[k]).wait_send()

            if n >= 14:
                @pl.when(is_root)
                def _():
                    remote(ref, ref, x2_s.at[p], x_r.at[n], sibling).wait_send()

            @pl.when(c == cr)
            def _():
                remote(ref, ref, c_s.at[n], x_r.at[n], sibling).wait_send()

    for d in range(2):
        half_copy(d).wait_recv()
        mid_copy(d).wait_recv()
        k = 2 if d == 0 else 6
        total = rows_of(k) + mid[d].astype(F32)
        for v in range(2):
            piece = total[:, v * 256:(v + 1) * 256]
            if v == d:
                piece = piece + half_mid[d].astype(F32)
            sb2[d, :, v * 256:(v + 1) * 256] = piece.astype(BF16)
        out_copy(k).start()

    pltpu.make_async_copy(rb.at[0], rb.at[0], o_r.at[0]).wait()
    total = rb[0].astype(F32)
    for k in (1, 7, 2, 6):
        out_copy(k).wait_recv()
        total = total + rb[k].astype(F32)
    out_ref[...] = total

    for d in range(2):
        mid_copy(d).wait_send()
        half_copy(d).wait_send()
    for k in (1, 7, 2, 6):
        out_copy(k).wait_send()

    @pl.when(jnp.logical_not(stays))
    def _():
        out_copy(0).wait_send()


def on_device(integrals, inverse_factor, energies, frequency):
    dma = pltpu.SemaphoreType.DMA
    vmem = pltpu.VMEM
    anywhere = pl.BlockSpec(memory_space=pl.ANY)
    return pl.pallas_call(
        kernel,
        out_shape=jax.ShapeDtypeStruct((64, 512), F32),
        in_specs=[
            anywhere,
            anywhere,
            pl.BlockSpec(memory_space=pltpu.VMEM),
            pl.BlockSpec(memory_space=pltpu.SMEM),
        ],
        out_specs=pl.BlockSpec(memory_space=pltpu.VMEM),
        scratch_shapes=[
            vmem((2, 8, 4, 64, 512), BF16),
            vmem((192, 4096), BF16),
            vmem((192, 512), F32),
            vmem((2, 4, 192, 512), BF16),
            vmem((2, 4, 192, 512), BF16),
            vmem((2, 6, 128), F32),
            vmem((2, 768, 128), F32),
            vmem((512, 512), F32),
            vmem((8, 64, 512), BF16),
            vmem((8, 64, 512), BF16),
            vmem((2, 64, 512), BF16),
            vmem((2, 64, 256), BF16),
            vmem((2, 64, 512), BF16),
            dma((2,)), dma((1,)), dma, dma,
            dma((2, 8, 2)), dma((2, 8, 2)), dma((2, 2, 4, 8)), dma((2, 2, 4, 8)),
            dma((2, 4, 4)), dma((2, 4, 4)), dma((2, 16)), dma((2,)), dma((16,)), dma((16,)),
            dma((2,)), dma((2,)), dma((2,)), dma((2,)), dma((8,)), dma((8,)),
        ],
        compiler_params=pltpu.CompilerParams(
            collective_id=0, has_side_effects=True, vmem_limit_bytes=60 * 1024 * 1024),
    )(integrals, inverse_factor.T, energies.reshape(6, 128), frequency)


def solution(mesh):
    return jax.shard_map(
        on_device,
        mesh=mesh,
        in_specs=(P(("pair", "col"), None), P("row", ("pair", "col")), P("pair"), P()),
        out_specs=P(("row", "pair"), "col"),
        check_vma=False,
    )
```

time: 94 us -> 88.1 us (0.937)
  the two profiles are of different devices: /device:TPU:5 before, /device:TPU:3 now
where the time goes in v3:
time: 88.1 us; the launch traced here: 87.9 us
  Pallas kernels  85.7 us (97%)
  local copies, waits for them, and re-layouts  1.57 us (2%)
    pallas_call x1, Pallas kernels, on_device(): pl.pallas_call(kernel, out_shape=jax.ShapeDtypeStruct((64, 512), F32), in...  85.7 us

profile of v3, /device:TPU:3, one launch (start us, length us, event | category | flops | bytes accessed | tf_op | source)
XLA Modules:
  0.0 87.9 jit_solution(6936321286196310540)
XLA Ops:
  0.7 85.7 %shard_map.46 = f32[64,512]{1,0:T(8,128)} custom-call(bf16[96,4096]{1,0:T(8,128)(2,1)} %i_ref.1, bf16[32,1024]{1,0:T(8,128)(2,1)} %bitcast.2, f32[6,128]{1,0:T(8,128)} %bitcast.3, f32[1]{0:T(128)S(6)} %copy.6.f_ref), custom_call_target="tpu_custom_call" | custom-call | tf_op jit(solution)/shard_map/pallas_call | solution.py:446
  86.3 1.6 %copy.7 = f32[64,512]{1,0:T(8,128)} copy(f32[64,512]{1,0:T(8,128)} %shard_map.46) | data formatting | bytes 262144

commit v4 on v3

v4 whole, which is shorter than its diff:
```python
import jax
import jax.numpy as jnp
from jax import lax
from jax.experimental import pallas as pl
from jax.experimental.pallas import tpu as pltpu
from jax.sharding import PartitionSpec as P

MESH = pl.DeviceIdType.MESH
F32, BF16 = jnp.float32, jnp.bfloat16


def rem(a, b):
    return lax.rem(a, jnp.int32(b))


def div(a, b):
    return lax.div(a, jnp.int32(b))


def device(x, y, z, c):
    return {"pair": rem(z, 2) * 8 + y, "row": x, "col": div(z, 2) * 2 + c}


def kernel(
    i_ref, l_ref, e_ref, f_ref, out_ref,
    lbuf, i2, tacc, tr, tc, eall, fcol, r, sb, rb, mid, half_mid, sb2,
    i_s, i_r, e_s, e_r,
    near_s, near_r, far_s, far_r,
    z_s, z_r, x_s, x2_s, c_s, x_r, m_s, m_r, h_s, h_r, o_s, o_r,
):
    pair, x, col = lax.axis_index("pair"), lax.axis_index("row"), lax.axis_index("col")
    zlo, y = div(pair, 8), rem(pair, 8)
    zhi, c = div(col, 2), rem(col, 2)
    z = zhi * 2 + zlo
    low = jnp.where(x == 3, 0, jnp.where(x == 0, 1, jnp.where(x == 2, 2, 3)))
    j = jnp.where(c == 0, low, 7 - low)

    def owner(block):
        low = jnp.where(block < 4, block, 7 - block)
        ox = jnp.where(low == 0, 3, jnp.where(low == 1, 0, jnp.where(low == 2, 2, 1)))
        return ox, jnp.where(block < 4, 0, 1)

    sibling = device(x, y, z, 1 - c)
    x_side = (device(rem(x + 1, 4), y, z, c), device(rem(x + 3, 4), y, z, c))
    y_side = (device(x, rem(y + 1, 8), z, c), device(x, rem(y + 7, 8), z, c))
    z_side = (device(x, y, rem(z + 1, 8), c), device(x, y, rem(z + 7, 8), c))
    z_pair = zhi * 2 + 1 - zlo
    px, pz, pc = div(j, 2), rem(j, 2), zlo
    stays = jnp.logical_and(px == x, jnp.logical_and(pz == zlo, pc == c))
    (sx, sc), sz = owner(2 * x + zlo), c

    def remote(src, dst, ssem, rsem, dev):
        return pltpu.make_async_remote_copy(
            src_ref=src, dst_ref=dst, send_sem=ssem, recv_sem=rsem,
            device_id=dev, device_id_type=MESH)

    keep_i = pltpu.make_async_copy(i_ref, i2.at[pl.ds(c * 96, 96), :], i_s.at[1])
    keep_i.start()

    def both(a, b):
        return jnp.logical_and(a, b)

    def either(a, b):
        return jnp.logical_or(a, b)

    barrier = pltpu.get_barrier_semaphore()

    def hello(dev):
        pl.semaphore_signal(barrier, inc=1, device_id_type=MESH, device_id=dev)

    def factor_target(t, k):
        ox, oc = owner(2 * x + t)
        return device(
            ox, rem(y + jnp.where(c == 0, k, 0), 8), rem(z + jnp.where(c == 1, k, 0), 8), oc)

    def factor_source(which, k):
        if which == 0:
            return device(div(j, 2), rem(y + 8 - k, 8), z, 0)
        return device(div(j, 2), y, rem(z + 8 - k, 8), 1)

    def own_block(t):
        ox, oc = owner(2 * x + t)
        return both(ox == x, oc == c)

    own_any = either(own_block(0), own_block(1))

    @pl.loop(1, 8)
    def _(k):
        for t in range(2):
            hello(factor_target(t, k))
            hello(factor_source(t, k))

    for t in range(2):
        @pl.when(jnp.logical_not(own_block(t)))
        def _():
            hello(factor_target(t, 0))

        @pl.when(either(div(j, 2) != x, c != t))
        def _():
            hello(factor_source(t, 0))

    for k in (6, 2, 7, 1):
        hello(device(px, rem(y + k, 8), zhi * 2 + pz, pc))
        hello(device(sx, rem(y + k, 8), zhi * 2 + sz, sc))
        hello(device(x, rem(y + k, 8), z, c))

    @pl.when(jnp.logical_not(stays))
    def _():
        hello(device(px, y, zhi * 2 + pz, pc))
        hello(device(sx, y, zhi * 2 + sz, sc))

    x_far = device(rem(x + 2, 4), y, z, c)
    for dev in (*x_side, x_far, sibling, *z_side):
        hello(dev)
    pl.semaphore_wait(
        barrier, 32 + 12 + 6 + jnp.where(stays, 0, 2) - jnp.where(own_any, 2, 0))

    def need(zl, yy):
        return zl * 4 + div(yy, 2) <= j

    def block(which, zl, yy, zh):
        return lbuf.at[zl, yy, zh, which * 32:which * 32 + 32, :]

    def factor_rows(t, k, act):
        src = l_ref.at[:, pl.ds(t * 512, 512)]
        dst = lbuf.at[zlo, y, zhi, pl.ds(c * 32, 32), :]
        needed = zlo * 4 + div(y, 2) <= 2 * x + t
        mine = both(own_block(t), k == 0)
        if act == "start":
            @pl.when(both(needed, mine))
            def _():
                pltpu.make_async_copy(src, dst, near_r.at[c, 0]).start()

        @pl.when(both(needed, jnp.logical_not(mine)))
        def _():
            copy = remote(src, dst, near_s.at[t, k], near_r.at[c, k], factor_target(t, k))
            if act == "start":
                copy.start()
            else:
                copy.wait_send()

    @pl.loop(0, 8)
    def _(i):
        k = rem(i + 2, 8)
        for t in range(2):
            factor_rows(t, k, "start")

    copy_e = remote(e_ref, eall.at[zlo], e_s, e_r, device(x, y, z_pair, c))
    copy_e.start()

    def near_wait(which, zl, yy, zh):
        ref = block(which, zl, yy, zh)
        k = rem(y + 8 - yy, 8) if which == 0 else rem(z + 8 - (2 * zh + zl), 8)

        @pl.when(need(zl, yy))
        def _():
            pltpu.make_async_copy(ref, ref, near_r.at[which, k]).wait()

    copy_i = remote(i_ref, i2.at[pl.ds(c * 96, 96), :], i_s.at[0], i_r.at[0], sibling)
    copy_i.start()

    def back(pos, s, d):
        return rem(pos + 8 - s, 8) if d == 0 else rem(pos + s, 8)

    def far(s, d, which, piece, cond, act):
        step = s + 1 if act == "recv" else s
        if which == 0:
            o = back(z, step, d)
            ok = rem(o, 2) * 4 + piece <= j
            ref = lbuf.at[rem(o, 2), pl.ds(2 * piece, 2), div(o, 2), 0:32, :]
            dev = z_side[d]
        else:
            o = back(y, step, d)
            zl, half = div(piece, 2), rem(piece, 2)
            ok = need(zl, o)
            ref = lbuf.at[zl, o, pl.ds(2 * half, 2), 32:64, :]
            dev = y_side[d]

        @pl.when(both(ok, cond))
        def _():
            copy = remote(
                ref, ref, far_s.at[which, d, s, piece], far_r.at[which, d, s, piece], dev)
            if act == "start":
                copy.start()
            elif act == "recv":
                copy.wait_recv()
            else:
                copy.wait_send()

    def goes(s, d, p):
        return either(s < 3, both(s == 3, p == d))

    @pl.loop(0, 4)
    def _(piece):
        for k in range(2):
            near_wait(0, zlo, 2 * piece + k, zhi)
        for d in range(2):
            far(0, d, 0, piece, True, "start")
        for k in range(2):
            near_wait(1, div(piece, 2), y, 2 * rem(piece, 2) + k)
        for d in range(2):
            far(0, d, 1, piece, True, "start")

    eall[zlo] = e_ref[...]
    copy_e.wait_recv()
    w = f_ref[0]
    for zl in range(2):
        e = eall[zl]
        fac = 2.0 * e / (e * e + w * w)
        for k in range(6):
            fcol[zl, k * 128:(k + 1) * 128, :] = jnp.broadcast_to(fac[k:k + 1, :], (128, 128)).T
    tacc[...] = jnp.zeros_like(tacc)
    r[...] = jnp.zeros_like(r)

    @pl.loop(1, 5)
    def _(s):
        @pl.loop(0, 4)
        def _(piece):
            for which in range(2):
                for d in range(2):
                    far(s - 1, d, which, piece, goes(s - 1, d, rem(piece, 2)), "recv")
                    far(s, d, which, piece, goes(s, d, rem(piece, 2)), "start")

    copy_i.wait_recv()
    keep_i.wait()

    @pl.loop(0, j + 1)
    def _(kt):
        left = i2[:, pl.ds(pl.multiple_of(kt * 512, 512), 512)]
        right = lbuf[div(kt, 4), pl.ds(2 * rem(kt, 4), 2)].reshape(512, 512)
        tacc[...] += jnp.dot(left, right, preferred_element_type=F32)

    tr[zlo, zhi] = tacc[...].astype(BF16)

    xr, cr = owner(z)
    dist = rem(x + 4 - xr, 4)
    is_root = both(dist == 0, c == cr)

    def part(buf, o, p):
        return buf.at[rem(o, 2), div(o, 2), p * 96:(p + 1) * 96, :]

    def small(o, q):
        return tr.at[rem(o, 2), div(o, 2), q * 48:(q + 1) * 48, :]

    def z_copy(s, d, q):
        ref = small(back(z, s, d), q)
        return remote(ref, ref, z_s.at[d, s, q], z_r.at[d, s, q], z_side[d])

    def z_wait(s, d, q):
        ref = small(back(z, s + 1, d), q)
        remote(ref, ref, z_s.at[d, s, q], z_r.at[d, s, q], z_side[d]).wait_recv()

    for q in range(4):
        for d in range(2):
            z_copy(0, d, q).start()

    def arrivals(s, act):
        for p in range(2):
            for d in range(2):
                @pl.when(both(either(s > 0, d == 0), either(s < 4, p == d)))
                def _():
                    act(s, p, d)

    def root_send(s, p, d):
        o, n = back(z, s, d), s * 4 + 2 * p + d

        @pl.when(s == 4)
        def _():
            remote(part(tr, o, p), part(tc, o, p), x2_s.at[p], x_r.at[n], x_far).start()

        for k in range(2):
            remote(part(tr, o, p), part(tc, o, p), x_s.at[k, n], x_r.at[n], x_side[k]).start()
        remote(part(tr, o, p), part(tc, o, p), c_s.at[n], x_r.at[n], sibling).start()
        pltpu.make_async_copy(part(tr, o, p), part(tc, o, p), x_r.at[n]).start()

    def x_wait(s, p, d):
        ref = part(tc, back(z, s, d), p)
        pltpu.make_async_copy(ref, ref, x_r.at[s * 4 + 2 * p + d]).wait()

    def relay(s, p, d):
        x_wait(s, p, d)
        ref, n = part(tc, back(z, s, d), p), s * 4 + 2 * p + d

        @pl.when(both(s < 4, dist == (1 if p == 0 else 3)))
        def _():
            remote(ref, ref, x_s.at[p, n], x_r.at[n], x_side[p]).start()

        remote(ref, ref, c_s.at[n], x_r.at[n], sibling).start()

    def relays(s):
        @pl.when(both(both(c == cr, rem(dist, 2) == 1), both(s >= 1, s <= 5)))
        def _():
            arrivals(s - 1, relay)

        @pl.when(both(both(c == cr, dist == 2), s >= 2))
        def _():
            arrivals(s - 2, relay)

    def add_chunks(first, last):
        @pl.loop(first, last)
        def _(i):
            h = div(i + 1, 2)
            o = jnp.where(rem(i, 2) == 1, rem(z + 8 - h, 8), rem(z + h, 8))
            zl, zh = rem(o, 2), div(o, 2)
            fac = fcol[zl, pl.ds(pl.multiple_of(zh * 192, 64), 192), :]
            fac = jnp.concatenate([fac] * 4, axis=1)
            rows = (fac * tr[zl, zh].astype(F32)).astype(BF16)
            r[...] += lax.dot_general(
                rows, tc[zl, zh], (((0,), (0,)), ((), ())), preferred_element_type=F32)

    def settle(first, last):
        @pl.when(either(c != cr, is_root))
        def _():
            @pl.loop(first, last)
            def _(s):
                arrivals(s, x_wait)

    copy_i.wait_send()
    copy_e.wait_send()

    @pl.loop(0, 8)
    def _(k):
        for t in range(2):
            factor_rows(t, k, "wait")

    @pl.loop(0, 4)
    def _(s):
        @pl.loop(0, 4)
        def _(piece):
            for which in range(2):
                for d in range(2):
                    far(s, d, which, piece, goes(s, d, rem(piece, 2)), "send")

    @pl.when(is_root)
    def _():
        for p in range(2):
            root_send(0, p, 0)

    @pl.loop(1, 5)
    def _(s):
        for p in range(2):
            for d in range(2):
                @pl.when(either(s < 4, p == d))
                def _():
                    for q in (2 * p, 2 * p + 1):
                        z_wait(s - 1, d, q)

                        @pl.when(goes(s, d, p))
                        def _():
                            z_copy(s, d, q).start()

                    @pl.when(is_root)
                    def _():
                        root_send(s, p, d)

        relays(s)

    settle(0, 3)
    add_chunks(0, 5)

    @pl.loop(5, 7)
    def _(s):
        relays(s)

    settle(3, 5)
    add_chunks(5, 8)

    def rows_of(k):
        return r[pl.ds(pl.multiple_of(rem(y + k, 8) * 64, 64), 64), :]

    def mid_copy(d):
        return remote(sb.at[3 if d == 0 else 5], mid.at[d], m_s.at[d], m_r.at[d], y_side[d])

    def half_copy(d):
        return remote(
            sb.at[4, :, d * 256:(d + 1) * 256], half_mid.at[d], h_s.at[d], h_r.at[d],
            device(x, rem(y + (2 if d == 0 else 6), 8), z, c))

    def out_copy(k):
        src = sb2.at[0 if k == 2 else 1] if k in (2, 6) else sb.at[k]
        return remote(
            src, rb.at[k], o_s.at[k], o_r.at[k], device(px, rem(y + k, 8), zhi * 2 + pz, pc))

    sb[4] = rows_of(4).astype(BF16)
    for d in range(2):
        half_copy(d).start()
    for d in range(2):
        sb[3 if d == 0 else 5] = rows_of(3 if d == 0 else 5).astype(BF16)
        mid_copy(d).start()
    for k in (1, 7):
        sb[k] = rows_of(k).astype(BF16)
        out_copy(k).start()
    sb[0] = rows_of(0).astype(BF16)

    @pl.when(stays)
    def _():
        pltpu.make_async_copy(sb.at[0], rb.at[0], o_r.at[0]).start()

    @pl.when(jnp.logical_not(stays))
    def _():
        out_copy(0).start()

    @pl.loop(0, 5)
    def _(s):
        for d in range(2):
            for q in range(4):
                @pl.when(goes(s, d, q // 2))
                def _():
                    z_copy(s, d, q).wait_send()

        def left(s, p, d):
            ref, n = part(tc, back(z, s, d), p), s * 4 + 2 * p + d
            for k in range(2):
                sent = is_root
                if k == p:
                    passed_on = both(both(c == cr, s < 4), dist == (1 if k == 0 else 3))
                    sent = either(is_root, passed_on)

                @pl.when(sent)
                def _():
                    remote(ref, ref, x_s.at[k, n], x_r.at[n], x_side[k]).wait_send()

            @pl.when(both(is_root, s == 4))
            def _():
                remote(ref, ref, x2_s.at[p], x_r.at[n], sibling).wait_send()

            @pl.when(c == cr)
            def _():
                remote(ref, ref, c_s.at[n], x_r.at[n], sibling).wait_send()

        arrivals(s, left)

    for d in range(2):
        half_copy(d).wait_recv()
        mid_copy(d).wait_recv()
        k = 2 if d == 0 else 6
        total = rows_of(k) + mid[d].astype(F32)
        for v in range(2):
            piece = total[:, v * 256:(v + 1) * 256]
            if v == d:
                piece = piece + half_mid[d].astype(F32)
            sb2[d, :, v * 256:(v + 1) * 256] = piece.astype(BF16)
        out_copy(k).start()

    pltpu.make_async_copy(rb.at[0], rb.at[0], o_r.at[0]).wait()
    total = rb[0].astype(F32)
    for k in (1, 7, 2, 6):
        out_copy(k).wait_recv()
        total = total + rb[k].astype(F32)
    out_ref[...] = total

    for d in range(2):
        mid_copy(d).wait_send()
        half_copy(d).wait_send()
    for k in (1, 7, 2, 6):
        out_copy(k).wait_send()

    @pl.when(jnp.logical_not(stays))
    def _():
        out_copy(0).wait_send()


def on_device(integrals, inverse_factor, energies, frequency):
    dma = pltpu.SemaphoreType.DMA
    vmem = pltpu.VMEM
    anywhere = pl.BlockSpec(memory_space=pl.ANY)
    return pl.pallas_call(
        kernel,
        out_shape=jax.ShapeDtypeStruct((64, 512), F32),
        in_specs=[
            anywhere,
            anywhere,
            pl.BlockSpec(memory_space=pltpu.VMEM),
            pl.BlockSpec(memory_space=pltpu.SMEM),
        ],
        out_specs=pl.BlockSpec(memory_space=pltpu.VMEM),
        scratch_shapes=[
            vmem((2, 8, 4, 64, 512), BF16),
            vmem((192, 4096), BF16),
            vmem((192, 512), F32),
            vmem((2, 4, 192, 512), BF16),
            vmem((2, 4, 192, 512), BF16),
            vmem((2, 6, 128), F32),
            vmem((2, 768, 128), F32),
            vmem((512, 512), F32),
            vmem((8, 64, 512), BF16),
            vmem((8, 64, 512), BF16),
            vmem((2, 64, 512), BF16),
            vmem((2, 64, 256), BF16),
            vmem((2, 64, 512), BF16),
            dma((2,)), dma((1,)), dma, dma,
            dma((2, 8)), dma((2, 8)), dma((2, 2, 4, 4)), dma((2, 2, 4, 4)),
            dma((2, 4, 4)), dma((2, 4, 4)), dma((2, 20)), dma((2,)), dma((20,)), dma((20,)),
            dma((2,)), dma((2,)), dma((2,)), dma((2,)), dma((8,)), dma((8,)),
        ],
        compiler_params=pltpu.CompilerParams(
            collective_id=0, has_side_effects=True, vmem_limit_bytes=60 * 1024 * 1024),
    )(integrals, inverse_factor.T, energies.reshape(6, 128), frequency)


def solution(mesh):
    return jax.shard_map(
        on_device,
        mesh=mesh,
        in_specs=(P(("pair", "col"), None), P("row", ("pair", "col")), P("pair"), P()),
        out_specs=P(("row", "pair"), "col"),
        check_vma=False,
    )
```

time: 88.1 us -> 85.9 us (0.975)
  the two profiles are of different devices: /device:TPU:3 before, /device:TPU:1 now
where the time goes in v4:
time: 85.9 us; the launch traced here: 85.6 us
  Pallas kernels  83.4 us (97%)
  local copies, waits for them, and re-layouts  1.57 us (2%)
    pallas_call x1, Pallas kernels, on_device(): pl.pallas_call(kernel, out_shape=jax.ShapeDtypeStruct((64, 512), F32), in...  83.4 us

profile of v4, /device:TPU:1, one launch (start us, length us, event | category | flops | bytes accessed | tf_op | source)
XLA Modules:
  0.0 85.6 jit_solution(13277880263067788950)
XLA Ops:
  0.7 83.4 %shard_map.46 = f32[64,512]{1,0:T(8,128)} custom-call(bf16[96,4096]{1,0:T(8,128)(2,1)} %i_ref.1, bf16[32,1024]{1,0:T(8,128)(2,1)} %bitcast.2, f32[6,128]{1,0:T(8,128)} %bitcast.3, f32[1]{0:T(128)S(6)} %copy.6.f_ref), custom_call_target="tpu_custom_call" | custom-call | tf_op jit(solution)/shard_map/pallas_call | solution.py:467
  84.1 1.6 %copy.7 = f32[64,512]{1,0:T(8,128)} copy(f32[64,512]{1,0:T(8,128)} %shard_map.46) | data formatting | bytes 262144

commit v5 on v4

--- a/solution.py
+++ b/solution.py
@@ -305,8 +305,9 @@
             fac = fcol[zl, pl.ds(pl.multiple_of(zh * 192, 64), 192), :]
             fac = jnp.concatenate([fac] * 4, axis=1)
             rows = (fac * tr[zl, zh].astype(F32)).astype(BF16)
-            r[...] += lax.dot_general(
+            product = lax.dot_general(
                 rows, tc[zl, zh], (((0,), (0,)), ((), ())), preferred_element_type=F32)
+            r[...] += product
 
     def settle(first, last):
         @pl.when(either(c != cr, is_root))
@@ -314,6 +315,11 @@
             @pl.loop(first, last)
             def _(s):
                 arrivals(s, x_wait)
+
+    @pl.when(is_root)
+    def _():
+        for p in range(2):
+            root_send(0, p, 0)
 
     copy_i.wait_send()
     copy_e.wait_send()
@@ -331,27 +337,23 @@
                 for d in range(2):
                     far(s, d, which, piece, goes(s, d, rem(piece, 2)), "send")
 
-    @pl.when(is_root)
-    def _():
-        for p in range(2):
-            root_send(0, p, 0)
-
     @pl.loop(1, 5)
     def _(s):
-        for p in range(2):
+        for q in range(4):
+            p = q // 2
             for d in range(2):
                 @pl.when(either(s < 4, p == d))
                 def _():
-                    for q in (2 * p, 2 * p + 1):
-                        z_wait(s - 1, d, q)
-
-                        @pl.when(goes(s, d, p))
+                    z_wait(s - 1, d, q)
+
+                    @pl.when(goes(s, d, p))
+                    def _():
+                        z_copy(s, d, q).start()
+
+                    if q % 2:
+                        @pl.when(is_root)
                         def _():
-                            z_copy(s, d, q).start()
-
-                    @pl.when(is_root)
-                    def _():
-                        root_send(s, p, d)
+                            root_send(s, p, d)
 
         relays(s)
 
@@ -463,13 +465,13 @@
 def on_device(integrals, inverse_factor, energies, frequency):
     dma = pltpu.SemaphoreType.DMA
     vmem = pltpu.VMEM
-    anywhere = pl.BlockSpec(memory_space=pl.ANY)
+    in_hbm = pl.BlockSpec(memory_space=pltpu.HBM)
     return pl.pallas_call(
         kernel,
         out_shape=jax.ShapeDtypeStruct((64, 512), F32),
         in_specs=[
-            anywhere,
-            anywhere,
+            in_hbm,
+            in_hbm,
             pl.BlockSpec(memory_space=pltpu.VMEM),
             pl.BlockSpec(memory_space=pltpu.SMEM),
         ],
@@ -494,7 +496,7 @@
             dma((2,)), dma((2,)), dma((2,)), dma((2,)), dma((8,)), dma((8,)),
         ],
         compiler_params=pltpu.CompilerParams(
-            collective_id=0, has_side_effects=True, vmem_limit_bytes=60 * 1024 * 1024),
+            collective_id=0, has_side_effects=True, vmem_limit_bytes=54528 * 1024),
     )(integrals, inverse_factor.T, energies.reshape(6, 128), frequency)
 
 

time: 85.9 us -> 83.7 us (0.974)
  Pallas kernels: 83.4 us -> 80.6 us
    pallas_call x1, Pallas kernels: 83.4 us -> 80.6 us  [on_device(): pl.pallas_call(kernel, out_shape=jax.ShapeDtypeStruct((64, 512), F32), in...]
where the time goes in v5:
time: 83.7 us; the launch traced here: 82.8 us
  Pallas kernels  80.6 us (96%)
  local copies, waits for them, and re-layouts  1.52 us (2%)
    pallas_call x1, Pallas kernels, on_device(): pl.pallas_call(kernel, out_shape=jax.ShapeDtypeStruct((64, 512), F32), in...  80.6 us

profile of v5, /device:TPU:1, one launch (start us, length us, event | category | flops | bytes accessed | tf_op | source)
XLA Modules:
  0.0 82.8 jit_solution(8086132206042855426)
XLA Ops:
  0.0 0.0 copy-start.1
  0.7 0.0 copy-done.1
  0.7 0.0 copy-start
  0.7 0.8 %copy-done = bf16[1024,32]{0,1:T(8,128)(2,1)S(1)} copy-done((bf16[1024,32]{0,1:T(8,128)(2,1)S(1)}, bf16[1024,32]{0,1:T(8,128)(2,1)}, u32[]{:S(2)}) %copy-start) | copy-done | bytes 65560
  1.5 80.6 %shard_map.46 = f32[64,512]{1,0:T(8,128)S(1)} custom-call(bf16[96,4096]{1,0:T(8,128)(2,1)} %i_ref.1, bf16[32,1024]{1,0:T(8,128)(2,1)S(1)} %bitcast.2, f32[6,128]{1,0:T(8,128)S(1)} %bitcast.3, f32[1]{0:T(128)S(6)} %copy.6.f_ref), custom_call_target="tpu_custom_call" | custom-call | tf_op jit(solution)/shard_map/pallas_call | solution.py:469
  82.1 0.7 copy.7
Async XLA Ops:
  0.0 0.7 copy-start.1
  0.7 0.8 %copy-start = (bf16[1024,32]{0,1:T(8,128)(2,1)S(1)}, bf16[1024,32]{0,1:T(8,128)(2,1)}, u32[]{:S(2)}) copy-start(bf16[1024,32]{0,1:T(8,128)(2,1)} %param.5) | copy-start | bytes 196612

commit v6 on v5

--- a/solution.py
+++ b/solution.py
@@ -68,19 +68,24 @@
     def hello(dev):
         pl.semaphore_signal(barrier, inc=1, device_id_type=MESH, device_id=dev)
 
+    def crosses(yy):
+        return rem(div(yy, 2), 2) == 1
+
     def factor_target(t, k):
         ox, oc = owner(2 * x + t)
         return device(
-            ox, rem(y + jnp.where(c == 0, k, 0), 8), rem(z + jnp.where(c == 1, k, 0), 8), oc)
+            ox, rem(y + jnp.where(c == 0, k, 0), 8),
+            jnp.where(c == 0, jnp.where(crosses(y), z_pair, z), rem(z + k, 8)), oc)
 
     def factor_source(which, k):
         if which == 0:
-            return device(div(j, 2), rem(y + 8 - k, 8), z, 0)
+            from_y = rem(y + 8 - k, 8)
+            return device(div(j, 2), from_y, jnp.where(crosses(from_y), z_pair, z), 0)
         return device(div(j, 2), y, rem(z + 8 - k, 8), 1)
 
     def own_block(t):
         ox, oc = owner(2 * x + t)
-        return both(ox == x, oc == c)
+        return both(both(ox == x, oc == c), either(c == 1, jnp.logical_not(crosses(y))))
 
     own_any = either(own_block(0), own_block(1))
 
@@ -95,7 +100,7 @@
         def _():
             hello(factor_target(t, 0))
 
-        @pl.when(either(div(j, 2) != x, c != t))
+        @pl.when(either(either(div(j, 2) != x, c != t), crosses(y) if t == 0 else False))
         def _():
             hello(factor_source(t, 0))
 
@@ -166,8 +171,9 @@
         step = s + 1 if act == "recv" else s
         if which == 0:
             o = back(z, step, d)
-            ok = rem(o, 2) * 4 + piece <= j
-            ref = lbuf.at[rem(o, 2), pl.ds(2 * piece, 2), div(o, 2), 0:32, :]
+            zl = jnp.where(rem(piece, 2) == 0, rem(o, 2), 1 - rem(o, 2))
+            ok = zl * 4 + piece <= j
+            ref = lbuf.at[zl, pl.ds(2 * piece, 2), div(o, 2), 0:32, :]
             dev = z_side[d]
         else:
             o = back(y, step, d)
@@ -193,7 +199,7 @@
     @pl.loop(0, 4)
     def _(piece):
         for k in range(2):
-            near_wait(0, zlo, 2 * piece + k, zhi)
+            near_wait(0, jnp.where(rem(piece, 2) == 0, zlo, 1 - zlo), 2 * piece + k, zhi)
         for d in range(2):
             far(0, d, 0, piece, True, "start")
         for k in range(2):

time: 83.7 us -> 83.4 us (level)
  no operation moved by 1% of the time
where the time goes in v6:
time: 83.4 us; the launch traced here: 82.4 us
  Pallas kernels  80.2 us (96%)
  local copies, waits for them, and re-layouts  1.52 us (2%)
    pallas_call x1, Pallas kernels, on_device(): pl.pallas_call(kernel, out_shape=jax.ShapeDtypeStruct((64, 512), F32), in...  80.2 us

profile of v6, /device:TPU:1, one launch (start us, length us, event | category | flops | bytes accessed | tf_op | source)
XLA Modules:
  0.0 82.4 jit_solution(10090948489938357284)
XLA Ops:
  0.0 0.0 copy-start.1
  0.7 0.0 copy-done.1
  0.7 0.0 copy-start
  0.7 0.8 %copy-done = bf16[1024,32]{0,1:T(8,128)(2,1)S(1)} copy-done((bf16[1024,32]{0,1:T(8,128)(2,1)S(1)}, bf16[1024,32]{0,1:T(8,128)(2,1)}, u32[]{:S(2)}) %copy-start) | copy-done | bytes 65560
  1.5 80.2 %shard_map.46 = f32[64,512]{1,0:T(8,128)S(1)} custom-call(bf16[96,4096]{1,0:T(8,128)(2,1)} %i_ref.1, bf16[32,1024]{1,0:T(8,128)(2,1)S(1)} %bitcast.2, f32[6,128]{1,0:T(8,128)S(1)} %bitcast.3, f32[1]{0:T(128)S(6)} %copy.6.f_ref), custom_call_target="tpu_custom_call" | custom-call | tf_op jit(solution)/shard_map/pallas_call | solution.py:475
  81.7 0.7 copy.7
Async XLA Ops:
  0.0 0.7 copy-start.1
  0.7 0.8 %copy-start = (bf16[1024,32]{0,1:T(8,128)(2,1)S(1)}, bf16[1024,32]{0,1:T(8,128)(2,1)}, u32[]{:S(2)}) copy-start(bf16[1024,32]{0,1:T(8,128)(2,1)} %param.5) | copy-start | bytes 196612

commit v7 on v6

--- a/solution.py
+++ b/solution.py
@@ -117,8 +117,10 @@
     x_far = device(rem(x + 2, 4), y, z, c)
     for dev in (*x_side, x_far, sibling, *z_side):
         hello(dev)
+    for k in (2, 6):
+        hello(device(x, y, rem(z + k, 8), c))
     pl.semaphore_wait(
-        barrier, 32 + 12 + 6 + jnp.where(stays, 0, 2) - jnp.where(own_any, 2, 0))
+        barrier, 32 + 12 + 8 + jnp.where(stays, 0, 2) - jnp.where(own_any, 2, 0))
 
     def need(zl, yy):
         return zl * 4 + div(yy, 2) <= j
@@ -168,19 +170,20 @@
         return rem(pos + 8 - s, 8) if d == 0 else rem(pos + s, 8)
 
     def far(s, d, which, piece, cond, act):
-        step = s + 1 if act == "recv" else s
+        step = s + 1 if act == "recv" else jnp.where(s == 3, 2, s)
+        ahead = jnp.where(s == 3, 2, 1)
         if which == 0:
             o = back(z, step, d)
             zl = jnp.where(rem(piece, 2) == 0, rem(o, 2), 1 - rem(o, 2))
             ok = zl * 4 + piece <= j
             ref = lbuf.at[zl, pl.ds(2 * piece, 2), div(o, 2), 0:32, :]
-            dev = z_side[d]
+            dev = device(x, y, back(z, ahead, 1 - d), c)
         else:
             o = back(y, step, d)
             zl, half = div(piece, 2), rem(piece, 2)
             ok = need(zl, o)
             ref = lbuf.at[zl, o, pl.ds(2 * half, 2), 32:64, :]
-            dev = y_side[d]
+            dev = device(x, back(y, ahead, 1 - d), z, c)
 
         @pl.when(both(ok, cond))
         def _():
@@ -225,7 +228,8 @@
             for which in range(2):
                 for d in range(2):
                     far(s - 1, d, which, piece, goes(s - 1, d, rem(piece, 2)), "recv")
-                    far(s, d, which, piece, goes(s, d, rem(piece, 2)), "start")
+                    far(s, d, which, piece, s < 3, "start")
+                    far(3, d, which, piece, both(s == 2, d == rem(piece, 2)), "start")
 
     copy_i.wait_recv()
     keep_i.wait()

time: 83.4 us -> 83.3 us (level)
  no operation moved by 1% of the time
where the time goes in v7:
time: 83.3 us; the launch traced here: 82.6 us
  Pallas kernels  80.4 us (97%)
  local copies, waits for them, and re-layouts  1.52 us (2%)
    pallas_call x1, Pallas kernels, on_device(): pl.pallas_call(kernel, out_shape=jax.ShapeDtypeStruct((64, 512), F32), in...  80.4 us

profile of v7, /device:TPU:1, one launch (start us, length us, event | category | flops | bytes accessed | tf_op | source)
XLA Modules:
  0.0 82.6 jit_solution(8777359103031473579)
XLA Ops:
  0.0 0.0 copy-start.1
  0.7 0.0 copy-done.1
  0.7 0.0 copy-start
  0.7 0.8 %copy-done = bf16[1024,32]{0,1:T(8,128)(2,1)S(1)} copy-done((bf16[1024,32]{0,1:T(8,128)(2,1)S(1)}, bf16[1024,32]{0,1:T(8,128)(2,1)}, u32[]{:S(2)}) %copy-start) | copy-done | bytes 65560
  1.5 80.4 %shard_map.46 = f32[64,512]{1,0:T(8,128)S(1)} custom-call(bf16[96,4096]{1,0:T(8,128)(2,1)} %i_ref.1, bf16[32,1024]{1,0:T(8,128)(2,1)S(1)} %bitcast.2, f32[6,128]{1,0:T(8,128)S(1)} %bitcast.3, f32[1]{0:T(128)S(6)} %copy.6.f_ref), custom_call_target="tpu_custom_call" | custom-call | tf_op jit(solution)/shard_map/pallas_call | solution.py:479
  81.9 0.7 copy.7
Async XLA Ops:
  0.0 0.7 copy-start.1
  0.7 0.8 %copy-start = (bf16[1024,32]{0,1:T(8,128)(2,1)S(1)}, bf16[1024,32]{0,1:T(8,128)(2,1)}, u32[]{:S(2)}) copy-start(bf16[1024,32]{0,1:T(8,128)(2,1)} %param.5) | copy-start | bytes 196612
